TPU v7x, 128 devices: a whole 4x4x4 slice. The times are simulated.
128 devices in a mesh: segment: 8 (over y_lo, z), dp: 16 (over y_hi, x, core).
Axes of the slice: x: 4, y: 4 (y_hi: 2, y_lo: 2; y = y_hi * 2 + y_lo), z: 4, core: 2. Of those that a mesh axis runs over, the one named last changes fastest.
Arguments:
- tokens: bfloat16 [4, 512, 6144], P(None, 'dp'), may hold values from -18 to 18
- norm_gain: bfloat16 [6144], replicated, may hold values from 0.099609375 to 1.8984375
- router_weight: bfloat16 [6144, 8], replicated, may hold values from -0.078125 to 0.078125
- expert_ids: int32 [4, 512, 2], P(None, 'dp'), may hold values from 0 to 7, all different within a row; in each aligned block of 32 rows (0 to 31, 32 to 63, ..., all dimensions but the last counted through in order) at most 12 rows name the same one
- w_gate: bfloat16 [8, 6144, 8192], P('segment', None, 'dp'), may hold values from -0.078125 to 0.078125
- w_up: bfloat16 [8, 6144, 8192], P('segment', None, 'dp'), may hold values from -0.078125 to 0.078125
- w_down: bfloat16 [8, 8192, 6144], P('segment', 'dp'), may hold values from -0.0625 to 0.0625
Outputs:
- scored: bfloat16 [4, 512, 6144], P(None, 'dp', 'segment')
Inputs may be any that keep to these rules, and one draw needn't show every extreme that they name: `expert_ids`: each token names two different experts. In each micro-batch the 32 rows of one device name each expert at most 12 times, and in every draw some expert is named exactly 12 times by some device's rows.
All inputs are finite; a program needn't handle non-finite values.
Results may differ from a plain program's by a relative error of at most 0.0035.
Values may be sent and summed in bfloat16 or wider, within the bound.
A program may use at most 128 MiB of HBM per device.

v0:
```python
import jax
import jax.numpy as jnp
from jax import lax
from jax.sharding import PartitionSpec as P

epsilon = 1e-05


def rms_normed(tokens, norm_gain):
    widened = tokens.astype(jnp.float32)
    inverse_rms = lax.rsqrt(jnp.mean(widened * widened, axis=-1, keepdims=True) + epsilon)
    return (widened, (widened * inverse_rms * norm_gain.astype(jnp.float32)).astype(jnp.bfloat16))


def pair_gates(pair_ids, logits):
    expert_range = jnp.arange(logits.shape[-1], dtype=jnp.int32)
    first_logit = jnp.sum(jnp.where(pair_ids[..., 0:1] == expert_range, logits, 0.0), axis=-1)
    second_logit = jnp.sum(jnp.where(pair_ids[..., 1:2] == expert_range, logits, 0.0), axis=-1)
    return (jax.nn.sigmoid(first_logit - second_logit), jax.nn.sigmoid(second_logit - first_logit))


def expert_weight(pair_ids, first_gate, second_gate, expert):
    return jnp.where(pair_ids[..., 0] == expert, first_gate, 0.0) + jnp.where(
        pair_ids[..., 1] == expert, second_gate, 0.0
    )


def slot_table(pair_ids, expert, slot_count):
    chosen = jnp.any(pair_ids == expert, axis=-1)
    hit_count = chosen.astype(jnp.int32)
    position = jnp.cumsum(hit_count, axis=-1) - hit_count
    slot_range = jnp.arange(slot_count, dtype=jnp.int32)
    dispatch = chosen[..., None, :] & (position[..., None, :] == slot_range[:, None])
    return (position, dispatch)


def per_device(tokens, norm_gain, router_weight, expert_ids, w_gate, w_up, w_down):
    micro_count, tok_rows, model_width = tokens.shape
    expert_count = router_weight.shape[1]
    slot_count = 2 * tok_rows // expert_count + tok_rows // 8
    segment_count = lax.axis_size("segment")
    segment_index = lax.axis_index("segment")
    slice_width = model_width // segment_count
    gate_matrix = w_gate[0]
    up_matrix = w_up[0]
    down_matrix = w_down[0]
    widened, normed = rms_normed(tokens, norm_gain)
    logits = jnp.dot(
        normed.reshape(-1, model_width), router_weight, preferred_element_type=jnp.float32
    )
    logits = logits.reshape(micro_count, tok_rows, expert_count)
    first_gate, second_gate = pair_gates(expert_ids, logits)
    outputs = []
    positions = []
    for micro_index in range(micro_count):
        position, dispatch = slot_table(expert_ids[micro_index], segment_index, slot_count)
        routed = jnp.dot(
            dispatch.astype(jnp.bfloat16), normed[micro_index], preferred_element_type=jnp.float32
        ).astype(jnp.bfloat16)
        piece_rows = lax.all_gather(routed, "dp", axis=0, tiled=True)
        gate_proj = jnp.dot(piece_rows, gate_matrix, preferred_element_type=jnp.float32)
        up_proj = jnp.dot(piece_rows, up_matrix, preferred_element_type=jnp.float32)
        hidden = (jax.nn.silu(gate_proj) * up_proj).astype(jnp.bfloat16)
        outputs.append(
            lax.psum_scatter(
                jnp.dot(hidden, down_matrix, preferred_element_type=jnp.float32),
                "dp",
                scatter_dimension=0,
                tiled=True,
            )
        )
        positions.append(position)
    own_part = lax.dynamic_slice_in_dim(widened, segment_index * slice_width, slice_width, 2)
    placed = []
    for micro_index in range(micro_count):
        weight = expert_weight(
            expert_ids[micro_index],
            first_gate[micro_index],
            second_gate[micro_index],
            segment_index,
        )
        taken = jnp.take(
            outputs[micro_index], jnp.clip(positions[micro_index], 0, slot_count - 1), axis=0
        )
        placed.append(weight[:, None] * taken)
    summed = lax.psum_scatter(jnp.stack(placed), "segment", scatter_dimension=2, tiled=True)
    return (own_part + summed).astype(jnp.bfloat16)


def solution(mesh):
    placed = (
        P(None, "dp", None),
        P(),
        P(),
        P(None, "dp", None),
        P("segment", None, "dp"),
        P("segment", None, "dp"),
        P("segment", "dp", None),
    )
    return jax.shard_map(
        per_device, mesh=mesh, in_specs=placed, out_specs=P(None, "dp", "segment"), check_vma=False
    )
```

profile of v0, /device:TPU:0, one launch (start us, length us, event | category | flops | bytes accessed | tf_op | source)
XLA Modules:
  0.0 637.2 jit_solution(11767465393413596786)
XLA Ops:
  17.9 50.2 %all-gather.13.cloned.1.call-done = bf16[16,12,6144]{2,1,0:T(8,128)(2,1)} async-done(((bf16[1,12,6144]{2,1,0:T(8,128)(2,1)}), bf16[16,12,6144]{2,1,0:T(8,128)(2,1)}) %all-gather.13.cloned.1.call-update) | async-done | bytes 2359312 | tf_op jit(solution)/shard_map/all_gather | solution.py:60
  70.9 50.7 %all-gather.9.cloned.1.call-done = bf16[16,12,6144]{2,1,0:T(8,128)(2,1)} async-done(((bf16[1,12,6144]{2,1,0:T(8,128)(2,1)}), bf16[16,12,6144]{2,1,0:T(8,128)(2,1)}) %all-gather.9.cloned.1.call-update) | async-done | bytes 2359312 | tf_op jit(solution)/shard_map/all_gather | solution.py:60
  125.9 49.3 %all-gather.11.cloned.1.call-done = bf16[16,12,6144]{2,1,0:T(8,128)(2,1)} async-done(((bf16[1,12,6144]{2,1,0:T(8,128)(2,1)}), bf16[16,12,6144]{2,1,0:T(8,128)(2,1)}) %all-gather.11.cloned.1.call-update) | async-done | bytes 2359312 | tf_op jit(solution)/shard_map/all_gather | solution.py:60
  175.2 4.3 reshape.193
  179.4 5.0 fusion.28
  184.5 4.5 fusion.30
  191.1 37.4 %all-gather.15.cloned.1.call-done = bf16[16,12,6144]{2,1,0:T(8,128)(2,1)} async-done(((bf16[1,12,6144]{2,1,0:T(8,128)(2,1)}), bf16[16,12,6144]{2,1,0:T(8,128)(2,1)}) %all-gather.15.cloned.1.call-update) | async-done | bytes 2359312 | tf_op jit(solution)/shard_map/all_gather | solution.py:60
  232.8 5.7 fusion.24
  238.5 10.2 %fusion.8 = f32[192,6144]{1,0:T(8,128)} fusion(bf16[1,512,6144]{2,1,0:T(8,128)(2,1)} %param.15, bf16[192,6144]{1,0:T(8,128)(2,1)} %reshape.197, bf16[1,6144,512]{2,1,0:T(8,128)(2,1)} %param.14, f32[192,512]{1,0:T(8,128)} %fusion.24), kind=kOutput, calls=%fused_computation.12 | convolution fusion | flops 2416508928 | bytes 20054016 | tf_op jit(solution)/shard_map/dot_general | solution.py:66
  248.7 9.6 %fusion.10 = f32[192,6144]{1,0:T(8,128)} fusion(bf16[1,512,6144]{2,1,0:T(8,128)(2,1)} %param.15, bf16[192,6144]{1,0:T(8,128)(2,1)S(1)} %reshape.195, bf16[1,6144,512]{2,1,0:T(8,128)(2,1)} %param.14, f32[192,512]{1,0:T(8,128)} %fusion.26), kind=kOutput, calls=%fused_computation.14 | convolution fusion | flops 2416508928 | bytes 20054016 | tf_op jit(solution)/shard_map/dot_general | solution.py:66
  258.3 10.4 %fusion.14 = f32[192,6144]{1,0:T(8,128)} fusion(bf16[1,512,6144]{2,1,0:T(8,128)(2,1)} %param.15, bf16[192,6144]{1,0:T(8,128)(2,1)} %reshape.191, bf16[1,6144,512]{2,1,0:T(8,128)(2,1)} %param.14, f32[192,512]{1,0:T(8,128)S(1)} %fusion.30), kind=kOutput, calls=%fused_computation.18 | convolution fusion | flops 2416508928 | bytes 20054016 | tf_op jit(solution)/shard_map/dot_general | solution.py:66
  268.7 9.5 %fusion.12 = f32[192,6144]{1,0:T(8,128)} fusion(bf16[1,512,6144]{2,1,0:T(8,128)(2,1)} %param.15, bf16[192,6144]{1,0:T(8,128)(2,1)S(1)} %copy-done.4, bf16[1,6144,512]{2,1,0:T(8,128)(2,1)} %param.14, f32[192,512]{1,0:T(8,128)S(1)} %fusion.28), kind=kOutput, calls=%fused_computation.16 | convolution fusion | flops 2416508928 | bytes 20054016 | tf_op jit(solution)/shard_map/dot_general | solution.py:66
  278.2 145.2 %fusion.122 = (f32[16,6144]{1,0:T(8,128)S(1)}, f32[16,6144]{1,0:T(8,128)S(1)}, f32[16,6144]{1,0:T(8,128)S(1)}, f32[16,6144]{1,0:T(8,128)S(1)}) fusion(f32[192,6144]{1,0:T(8,128)} %fusion.8, f32[192,6144]{1,0:T(8,128)} %fusion.10, f32[192,6144]{1,0:T(8,128)} %fusion.12, f32[192,6144]{1,0:T(8,128)} %fusion.14), kind=kCustom, calls=%all-reduce-scatter.4 | all-reduce-scatter fusion | flops 6291457 | bytes 20447744
  430.3 5.2 collective-permute-start.15
  438.2 12.9 %collective-permute-done.15 = f32[12,6144]{1,0:T(8,128)S(1)} collective-permute-done((f32[12,6144]{1,0:T(8,128)S(1)}, f32[12,6144]{1,0:T(8,128)S(1)}, u32[]{:S(2)}, u32[]{:S(2)}) %collective-permute-start.15) | collective-permute-done | bytes 294944
  453.2 6.9 %collective-permute-start.8 = (f32[16,6144]{1,0:T(8,128)S(1)}, f32[16,6144]{1,0:T(8,128)}, u32[]{:S(2)}, u32[]{:S(2)}) collective-permute-start(f32[16,6144]{1,0:T(8,128)S(1)} %get-tuple-element.17), channel_id=1, source_target_pairs={{0,1},{1,2},{2,3},{3,4},{4,5},{5,6},{6,7},{7,8},{8,9},{9,10},{10,1... | collective-permute-start | bytes 1179656
  460.1 4.8 collective-permute-start.6
  465.0 8.2 %collective-permute-start.11 = (f32[12,6144]{1,0:T(8,128)S(1)}, f32[12,6144]{1,0:T(8,128)}, u32[]{:S(2)}, u32[]{:S(2)}) collective-permute-start(f32[12,6144]{1,0:T(8,128)S(1)} %slice.122), channel_id=1, source_target_pairs={{0,4},{1,5},{2,6},{3,7},{4,8},{5,9},{6,10},{7,11},{8,12},{9,13},{1... | collective-permute-start | bytes 884744
  473.2 18.5 %concatenate.3 = f32[76,6144]{1,0:T(8,128)} concatenate(f32[12,6144]{1,0:T(8,128)} %copy-done.5, f32[16,6144]{1,0:T(8,128)S(1)} %collective-permute-done.14, f32[16,6144]{1,0:T(8,128)} %collective-permute-done.13, f32[16,6144]{1,0:T(8,128)} %collective-permute-done.12, f32[16,6144]{1,0:T(8,128)S(1)} %get-tuple-element.16), dimensions={0} | concatenate | bytes 3735552
  500.1 6.9 %collective-permute-start.7 = (f32[12,6144]{1,0:T(8,128)S(1)}, f32[12,6144]{1,0:T(8,128)}, u32[]{:S(2)}, u32[]{:S(2)}) collective-permute-start(f32[12,6144]{1,0:T(8,128)S(1)} %slice.121), channel_id=1, source_target_pairs={{0,4},{1,5},{2,6},{3,7},{4,8},{5,9},{6,10},{7,11},{8,12},{9,13},{1... | collective-permute-start | bytes 884744
  507.0 18.8 %concatenate.2 = f32[76,6144]{1,0:T(8,128)} concatenate(f32[12,6144]{1,0:T(8,128)} %collective-permute-done.11, f32[16,6144]{1,0:T(8,128)} %collective-permute-done.10, f32[16,6144]{1,0:T(8,128)} %collective-permute-done.9, f32[16,6144]{1,0:T(8,128)} %collective-permute-done.8, f32[16,6144]{1,0:T(8,128)S(1)} %get-tuple-element.17), dimensions={0} | concatenate | bytes 3735552
  534.3 18.5 %concatenate.1 = f32[76,6144]{1,0:T(8,128)} concatenate(f32[12,6144]{1,0:T(8,128)} %collective-permute-done.7, f32[16,6144]{1,0:T(8,128)} %collective-permute-done.6, f32[16,6144]{1,0:T(8,128)S(1)} %collective-permute-done.5, f32[16,6144]{1,0:T(8,128)} %collective-permute-done.4, f32[16,6144]{1,0:T(8,128)S(1)} %get-tuple-element.18), dimensions={0} | concatenate | bytes 3735552
  554.0 18.3 %concatenate = f32[76,6144]{1,0:T(8,128)} concatenate(f32[12,6144]{1,0:T(8,128)} %collective-permute-done.3, f32[16,6144]{1,0:T(8,128)S(1)} %collective-permute-done.2, f32[16,6144]{1,0:T(8,128)S(1)} %collective-permute-done.1, f32[16,6144]{1,0:T(8,128)} %collective-permute-done, f32[16,6144]{1,0:T(8,128)S(1)} %get-tuple-element.19), dimensions={0} | concatenate | bytes 3735552
  584.4 44.4 %reduce-scatter.10.cloned.1.call-done = f32[4,32,768]{2,1,0:T(8,128)} async-done(((f32[4,32,6144]{2,1,0:T(8,128)}), f32[4,32,768]{2,1,0:T(8,128)}) %reduce-scatter.10.cloned.1.call-update) | async-done | bytes 393232 | tf_op jit(solution)/shard_map/reduce_scatter | solution.py:86
  (117 shorter events, 67.5 us)
Async XLA Ops:
  6.5 61.5 %all-gather.13.cloned.1.call-start = ((), (), s32[]{:S(2)}) async-start(), calls=%async_computation.4 | async-start | bytes 3342336 | tf_op jit(solution)/shard_map/all_gather | solution.py:60
  13.2 108.4 %all-gather.9.cloned.1.call-start = ((), (), s32[]{:S(2)}) async-start(), calls=%async_computation.2 | async-start | bytes 3342336 | tf_op jit(solution)/shard_map/all_gather | solution.py:60
  14.7 160.4 %all-gather.11.cloned.1.call-start = ((), (), s32[]{:S(2)}) async-start(), calls=%async_computation.3 | async-start | bytes 3342336 | tf_op jit(solution)/shard_map/all_gather | solution.py:60
  15.7 212.9 %all-gather.15.cloned.1.call-start = ((), (), s32[]{:S(2)}) async-start(), calls=%async_computation.5 | async-start | bytes 3342336 | tf_op jit(solution)/shard_map/all_gather | solution.py:60
  16.6 612.3 %reduce-scatter.10.cloned.1.call-start = ((), (), s32[]{:S(2)}) async-start(), calls=%async_computation.1 | async-start | bytes 3538944 | tf_op jit(solution)/shard_map/reduce_scatter | solution.py:86
  278.2 150.8 %copy-start.7 = (u32[128]{0:T(128)S(1)}, u32[128]{0:T(128)}, u32[]{:S(2)}) copy-start(u32[128]{0:T(128)} %constant.51) | copy-start | bytes 1540
  423.4 29.8 %collective-permute-start.14 = (f32[16,6144]{1,0:T(8,128)S(1)}, f32[16,6144]{1,0:T(8,128)S(1)}, u32[]{:S(2)}, u32[]{:S(2)}) collective-permute-start(f32[16,6144]{1,0:T(8,128)S(1)} %get-tuple-element.16), channel_id=1, source_target_pairs={{0,3},{1,4},{2,5},{3,6},{4,7},{5,8},{6,9},{7,10},{8,11},{9,12},{10... | collective-permute-start | bytes 1179656
  424.7 35.4 %collective-permute-start.13 = (f32[16,6144]{1,0:T(8,128)S(1)}, f32[16,6144]{1,0:T(8,128)}, u32[]{:S(2)}, u32[]{:S(2)}) collective-permute-start(f32[16,6144]{1,0:T(8,128)S(1)} %get-tuple-element.16), channel_id=1, source_target_pairs={{0,2},{1,3},{2,4},{3,5},{4,6},{5,7},{6,8},{7,9},{8,10},{9,11},{10,... | collective-permute-start | bytes 1179656
  426.8 38.2 %collective-permute-start.12 = (f32[16,6144]{1,0:T(8,128)S(1)}, f32[16,6144]{1,0:T(8,128)}, u32[]{:S(2)}, u32[]{:S(2)}) collective-permute-start(f32[16,6144]{1,0:T(8,128)S(1)} %get-tuple-element.16), channel_id=1, source_target_pairs={{0,1},{1,2},{2,3},{3,4},{4,5},{5,6},{6,7},{7,8},{8,9},{9,10},{10,1... | collective-permute-start | bytes 1179656
  430.3 20.9 %collective-permute-start.15 = (f32[12,6144]{1,0:T(8,128)S(1)}, f32[12,6144]{1,0:T(8,128)S(1)}, u32[]{:S(2)}, u32[]{:S(2)}) collective-permute-start(f32[12,6144]{1,0:T(8,128)S(1)} %slice.123), channel_id=1, source_target_pairs={{0,4},{1,5},{2,6},{3,7},{4,8},{5,9},{6,10},{7,11},{8,12},{9,13},{1... | collective-permute-start | bytes 884744
  435.6 59.0 %collective-permute-start.10 = (f32[16,6144]{1,0:T(8,128)S(1)}, f32[16,6144]{1,0:T(8,128)}, u32[]{:S(2)}, u32[]{:S(2)}) collective-permute-start(f32[16,6144]{1,0:T(8,128)S(1)} %get-tuple-element.17), channel_id=1, source_target_pairs={{0,3},{1,4},{2,5},{3,6},{4,7},{5,8},{6,9},{7,10},{8,11},{9,12},{10... | collective-permute-start | bytes 1179656
  451.1 13.8 %copy-start.5 = (f32[12,6144]{1,0:T(8,128)}, f32[12,6144]{1,0:T(8,128)S(1)}, u32[]{:S(2)}) copy-start(f32[12,6144]{1,0:T(8,128)S(1)} %collective-permute-done.15) | copy-start | bytes 884740
  451.1 45.5 %collective-permute-start.9 = (f32[16,6144]{1,0:T(8,128)S(1)}, f32[16,6144]{1,0:T(8,128)}, u32[]{:S(2)}, u32[]{:S(2)}) collective-permute-start(f32[16,6144]{1,0:T(8,128)S(1)} %get-tuple-element.17), channel_id=1, source_target_pairs={{0,2},{1,3},{2,4},{3,5},{4,6},{5,7},{6,8},{7,9},{8,10},{9,11},{10,... | collective-permute-start | bytes 1179656
  453.2 46.9 %collective-permute-start.8 = (f32[16,6144]{1,0:T(8,128)S(1)}, f32[16,6144]{1,0:T(8,128)}, u32[]{:S(2)}, u32[]{:S(2)}) collective-permute-start(f32[16,6144]{1,0:T(8,128)S(1)} %get-tuple-element.17), channel_id=1, source_target_pairs={{0,1},{1,2},{2,3},{3,4},{4,5},{5,6},{6,7},{7,8},{8,9},{9,10},{10,1... | collective-permute-start | bytes 1179656
  460.1 68.5 %collective-permute-start.6 = (f32[16,6144]{1,0:T(8,128)S(1)}, f32[16,6144]{1,0:T(8,128)}, u32[]{:S(2)}, u32[]{:S(2)}) collective-permute-start(f32[16,6144]{1,0:T(8,128)S(1)} %get-tuple-element.18), channel_id=1, source_target_pairs={{0,3},{1,4},{2,5},{3,6},{4,7},{5,8},{6,9},{7,10},{8,11},{9,12},{10... | collective-permute-start | bytes 1179656
  465.0 27.9 %collective-permute-start.11 = (f32[12,6144]{1,0:T(8,128)S(1)}, f32[12,6144]{1,0:T(8,128)}, u32[]{:S(2)}, u32[]{:S(2)}) collective-permute-start(f32[12,6144]{1,0:T(8,128)S(1)} %slice.122), channel_id=1, source_target_pairs={{0,4},{1,5},{2,6},{3,7},{4,8},{5,9},{6,10},{7,11},{8,12},{9,13},{1... | collective-permute-start | bytes 884744
  492.8 38.1 %collective-permute-start.5 = (f32[16,6144]{1,0:T(8,128)S(1)}, f32[16,6144]{1,0:T(8,128)S(1)}, u32[]{:S(2)}, u32[]{:S(2)}) collective-permute-start(f32[16,6144]{1,0:T(8,128)S(1)} %get-tuple-element.18), channel_id=1, source_target_pairs={{0,2},{1,3},{2,4},{3,5},{4,6},{5,7},{6,8},{7,9},{8,10},{9,11},{10,... | collective-permute-start | bytes 1179656
  494.6 39.7 %collective-permute-start.4 = (f32[16,6144]{1,0:T(8,128)S(1)}, f32[16,6144]{1,0:T(8,128)}, u32[]{:S(2)}, u32[]{:S(2)}) collective-permute-start(f32[16,6144]{1,0:T(8,128)S(1)} %get-tuple-element.18), channel_id=1, source_target_pairs={{0,1},{1,2},{2,3},{3,4},{4,5},{5,6},{6,7},{7,8},{8,9},{9,10},{10,1... | collective-permute-start | bytes 1179656
  496.7 57.2 %collective-permute-start.2 = (f32[16,6144]{1,0:T(8,128)S(1)}, f32[16,6144]{1,0:T(8,128)S(1)}, u32[]{:S(2)}, u32[]{:S(2)}) collective-permute-start(f32[16,6144]{1,0:T(8,128)S(1)} %get-tuple-element.19), channel_id=1, source_target_pairs={{0,3},{1,4},{2,5},{3,6},{4,7},{5,8},{6,9},{7,10},{8,11},{9,12},{10... | collective-permute-start | bytes 1179656
  500.1 26.8 %collective-permute-start.7 = (f32[12,6144]{1,0:T(8,128)S(1)}, f32[12,6144]{1,0:T(8,128)}, u32[]{:S(2)}, u32[]{:S(2)}) collective-permute-start(f32[12,6144]{1,0:T(8,128)S(1)} %slice.121), channel_id=1, source_target_pairs={{0,4},{1,5},{2,6},{3,7},{4,8},{5,9},{6,10},{7,11},{8,12},{9,13},{1... | collective-permute-start | bytes 884744
  526.9 27.0 %collective-permute-start.1 = (f32[16,6144]{1,0:T(8,128)S(1)}, f32[16,6144]{1,0:T(8,128)S(1)}, u32[]{:S(2)}, u32[]{:S(2)}) collective-permute-start(f32[16,6144]{1,0:T(8,128)S(1)} %get-tuple-element.19), channel_id=1, source_target_pairs={{0,2},{1,3},{2,4},{3,5},{4,6},{5,7},{6,8},{7,9},{8,10},{9,11},{10,... | collective-permute-start | bytes 1179656
  528.6 25.3 %collective-permute-start = (f32[16,6144]{1,0:T(8,128)S(1)}, f32[16,6144]{1,0:T(8,128)}, u32[]{:S(2)}, u32[]{:S(2)}) collective-permute-start(f32[16,6144]{1,0:T(8,128)S(1)} %get-tuple-element.19), channel_id=1, source_target_pairs={{0,1},{1,2},{2,3},{3,4},{4,5},{5,6},{6,7},{7,8},{8,9},{9,10},{10,1... | collective-permute-start | bytes 1179656
  530.9 23.0 %collective-permute-start.3 = (f32[12,6144]{1,0:T(8,128)S(1)}, f32[12,6144]{1,0:T(8,128)}, u32[]{:S(2)}, u32[]{:S(2)}) collective-permute-start(f32[12,6144]{1,0:T(8,128)S(1)} %slice.120), channel_id=1, source_target_pairs={{0,4},{1,5},{2,6},{3,7},{4,8},{5,9},{6,10},{7,11},{8,12},{9,13},{1... | collective-permute-start | bytes 884744
  582.4 48.3 %copy-start.1 = (bf16[6144,8]{0,1:T(8,128)(2,1)S(1)}, bf16[6144,8]{0,1:T(8,128)(2,1)}, u32[]{:S(2)}) copy-start(bf16[6144,8]{0,1:T(8,128)(2,1)} %param.11) | copy-start | bytes 294916
  (7 other events, 47.3 us)
Sparse Core Ops, SparseCore 0:
  13.3 54.7 all-gather.12
  70.5 51.0 all-gather.8
  124.1 51.0 all-gather.10
  177.5 51.0 all-gather.14
  581.2 47.6 reduce-scatter.9
where the time goes:
time: 641 us; the launch traced here: 637 us
  waiting for transfers between devices  245 us (38%)
  blocking collectives  145 us (23%)
  local copies, waits for them, and re-layouts  101 us (16%)
  matrix products  61.6 us (10%)
  starting transfers between devices  57.1 us (9%)
  between operations  14.2 us (2%)
  other arithmetic  13.3 us (2%)
    all_gather x4, waiting for transfers between devices, per_device(): piece_rows = lax.all_gather(routed, 'dp', axis=0, tiled=True)  188 us
    unnamed x1, blocking collectives  145 us
    unnamed x37, local copies, waits for them, and re-layouts  96.3 us
    unnamed x16, starting transfers between devices  56.9 us
    reduce_scatter x1, waiting for transfers between devices, per_device(): lax.psum_scatter(jnp.stack(placed), 'segment', scatter_dimension=2, tiled...  44.4 us
    dot_general x4, matrix products, per_device(): jnp.dot(hidden, down_matrix, preferred_element_type=jnp.float32)  39.7 us
    dot_general x4, matrix products, per_device(): jnp.dot(piece_rows, gate_matrix, preferred_element_type=jnp.float32)  17.3 us
    unnamed x21, waiting for transfers between devices  13 us
  transfers between devices with their start and end apart: 21, of which 6 were waited for; matrix products, arithmetic and copies ran while one was open for 14% of the time, Pallas kernels for 0%

commit v1 on v0

--- a/solution.py
+++ b/solution.py
@@ -57,7 +57,9 @@
         routed = jnp.dot(
             dispatch.astype(jnp.bfloat16), normed[micro_index], preferred_element_type=jnp.float32
         ).astype(jnp.bfloat16)
-        piece_rows = lax.all_gather(routed, "dp", axis=0, tiled=True)
+        piece_rows = jnp.concatenate(
+            lax.all_to_all(jnp.stack([routed] * lax.axis_size("dp")), "dp", 0, 0), axis=0
+        )
         gate_proj = jnp.dot(piece_rows, gate_matrix, preferred_element_type=jnp.float32)
         up_proj = jnp.dot(piece_rows, up_matrix, preferred_element_type=jnp.float32)
         hidden = (jax.nn.silu(gate_proj) * up_proj).astype(jnp.bfloat16)

time: 641 us -> 598 us (0.933)
  waiting for transfers between devices: 245 us -> 164 us
  starting transfers between devices: 57.1 us -> 89.2 us
    all_gather x4 -> x0, waiting for transfers between devices: 188 us -> none  [per_device(): piece_rows = lax.all_gather(routed, 'dp', axis=0, tiled=True)]
    all_to_all x0 -> x4, waiting for transfers between devices: none -> 110 us  [per_device(): lax.all_to_all(jnp.stack([routed] * lax.axis_size('dp')), 'dp', 0, 0)]
    all_to_all x0 -> x4, starting transfers between devices: none -> 25 us  [per_device(): lax.all_to_all(jnp.stack([routed] * lax.axis_size('dp')), 'dp', 0, 0)]
    unnamed x37 -> x31, local copies, waits for them, and re-layouts: 96.3 us -> 80.7 us
    reshape x0 -> x4, local copies, waits for them, and re-layouts: none -> 13.6 us  [per_device(): jnp.concatenate(lax.all_to_all(jnp.stack([routed] * lax.axis_size('dp')),...]
    another operation x0 -> x4, local copies, waits for them, and re-layouts: none -> 8.13 us  [per_device(): jnp.stack([routed] * lax.axis_size('dp'))]
    unnamed x16, starting transfers between devices: 56.9 us -> 64 us
    unnamed x21 -> x17, waiting for transfers between devices: 13 us -> 10.8 us
  transfers between devices with their start and end apart: 21 -> 21, of which waited for: 6 -> 6; matrix products, arithmetic and copies ran while one was open for 14% -> 20% of each run, Pallas kernels for 0% -> 0%
where the time goes in v1:
time: 598 us; the launch traced here: 594 us
  waiting for transfers between devices  164 us (27%)
  blocking collectives  145 us (24%)
  local copies, waits for them, and re-layouts  107 us (18%)
  starting transfers between devices  89.2 us (15%)
  matrix products  61.3 us (10%)
  between operations  14.5 us (2%)
  other arithmetic  13.3 us (2%)
    unnamed x1, blocking collectives  145 us
    all_to_all x4, waiting for transfers between devices, per_device(): lax.all_to_all(jnp.stack([routed] * lax.axis_size('dp')), 'dp', 0, 0)  110 us
    unnamed x31, local copies, waits for them, and re-layouts  80.7 us
    unnamed x16, starting transfers between devices  64 us
    reduce_scatter x1, waiting for transfers between devices, per_device(): lax.psum_scatter(jnp.stack(placed), 'segment', scatter_dimension=2, tiled...  42.9 us
    dot_general x4, matrix products, per_device(): jnp.dot(hidden, down_matrix, preferred_element_type=jnp.float32)  39.5 us
    all_to_all x4, starting transfers between devices, per_device(): lax.all_to_all(jnp.stack([routed] * lax.axis_size('dp')), 'dp', 0, 0)  25 us
    dot_general x4, matrix products, per_device(): jnp.dot(piece_rows, gate_matrix, preferred_element_type=jnp.float32)  19.9 us
  transfers between devices with their start and end apart: 21, of which 6 were waited for; matrix products, arithmetic and copies ran while one was open for 20% of the time, Pallas kernels for 0%

profile of v1, /device:TPU:0, one launch (start us, length us, event | category | flops | bytes accessed | tf_op | source)
XLA Modules:
  0.0 594.4 jit_solution(9140829957652679538)
XLA Ops:
  14.5 7.2 %all-to-all-start = ((bf16[16,12,6144]{2,1,0:T(8,128)(2,1)}), bf16[16,12,6144]{2,1,0:T(8,128)(2,1)}, u32[]{:S(2)}, u32[]{:S(2)}) async-start(bf16[16,12,6144]{2,1,0:T(8,128)(2,1)} %stack.18), calls=%async_computation | async-start | bytes 6291456 | tf_op jit(solution)/shard_map/all_to_all | solution.py:61
  21.9 42.2 %all-to-all-done = bf16[16,12,6144]{2,1,0:T(8,128)(2,1)} async-done(((bf16[16,12,6144]{2,1,0:T(8,128)(2,1)}), bf16[16,12,6144]{2,1,0:T(8,128)(2,1)}, u32[]{:S(2)}, u32[]{:S(2)}) %all-to-all-start) | async-done | bytes 2359328 | tf_op jit(solution)/shard_map/all_to_all | solution.py:61
  66.1 6.1 %all-to-all-start.1 = ((bf16[16,12,6144]{2,1,0:T(8,128)(2,1)}), bf16[16,12,6144]{2,1,0:T(8,128)(2,1)}, u32[]{:S(2)}, u32[]{:S(2)}) async-start(bf16[16,12,6144]{2,1,0:T(8,128)(2,1)} %stack.20), calls=%async_computation.1 | async-start | bytes 6291456 | tf_op jit(solution)/shard_map/all_to_all | solution.py:61
  74.4 40.2 %all-to-all-done.1 = bf16[16,12,6144]{2,1,0:T(8,128)(2,1)} async-done(((bf16[16,12,6144]{2,1,0:T(8,128)(2,1)}), bf16[16,12,6144]{2,1,0:T(8,128)(2,1)}, u32[]{:S(2)}, u32[]{:S(2)}) %all-to-all-start.1) | async-done | bytes 2359328 | tf_op jit(solution)/shard_map/all_to_all | solution.py:61
  116.6 5.9 all-to-all-start.2
  141.8 10.2 %fusion.10 = f32[192,6144]{1,0:T(8,128)} fusion(bf16[1,512,6144]{2,1,0:T(8,128)(2,1)} %param.15, bf16[192,6144]{1,0:T(8,128)(2,1)} %reshape.167, bf16[1,6144,512]{2,1,0:T(8,128)(2,1)} %param.14, f32[192,512]{1,0:T(8,128)} %fusion.26), kind=kOutput, calls=%fused_computation.14 | convolution fusion | flops 2416508928 | bytes 20054016 | tf_op jit(solution)/shard_map/dot_general | solution.py:68
  152.1 12.8 %all-to-all-done.2 = bf16[16,12,6144]{2,1,0:T(8,128)(2,1)S(1)} async-done(((bf16[16,12,6144]{2,1,0:T(8,128)(2,1)}), bf16[16,12,6144]{2,1,0:T(8,128)(2,1)S(1)}, u32[]{:S(2)}, u32[]{:S(2)}) %all-to-all-start.2) | async-done | bytes 2359328 | tf_op jit(solution)/shard_map/all_to_all | solution.py:61
  166.9 5.8 all-to-all-start.3
  180.2 9.6 %fusion.8 = f32[192,6144]{1,0:T(8,128)} fusion(bf16[1,512,6144]{2,1,0:T(8,128)(2,1)} %param.15, bf16[192,6144]{1,0:T(8,128)(2,1)S(1)} %copy-done.4, bf16[1,6144,512]{2,1,0:T(8,128)(2,1)} %param.14, f32[192,512]{1,0:T(8,128)S(1)} %copy-done.6), kind=kOutput, calls=%fused_computation.12 | convolution fusion | flops 2416508928 | bytes 20054016 | tf_op jit(solution)/shard_map/dot_general | solution.py:68
  189.8 10.2 %fusion.6 = f32[192,6144]{1,0:T(8,128)} fusion(bf16[1,512,6144]{2,1,0:T(8,128)(2,1)} %param.15, bf16[192,6144]{1,0:T(8,128)(2,1)} %reshape.171, bf16[1,6144,512]{2,1,0:T(8,128)(2,1)} %param.14, f32[192,512]{1,0:T(8,128)S(1)} %fusion.22), kind=kOutput, calls=%fused_computation.10 | convolution fusion | flops 2416508928 | bytes 20054016 | tf_op jit(solution)/shard_map/dot_general | solution.py:68
  200.0 15.1 %all-to-all-done.3 = bf16[16,12,6144]{2,1,0:T(8,128)(2,1)} async-done(((bf16[16,12,6144]{2,1,0:T(8,128)(2,1)}), bf16[16,12,6144]{2,1,0:T(8,128)(2,1)}, u32[]{:S(2)}, u32[]{:S(2)}) %all-to-all-start.3) | async-done | bytes 2359328 | tf_op jit(solution)/shard_map/all_to_all | solution.py:61
  222.1 9.5 %fusion.4 = f32[192,6144]{1,0:T(8,128)} fusion(bf16[1,512,6144]{2,1,0:T(8,128)(2,1)} %param.15, bf16[192,6144]{1,0:T(8,128)(2,1)S(1)} %reshape.173, bf16[1,6144,512]{2,1,0:T(8,128)(2,1)} %param.14, f32[192,512]{1,0:T(8,128)S(1)} %fusion.20), kind=kOutput, calls=%fused_computation.8 | convolution fusion | flops 2416508928 | bytes 20054016 | tf_op jit(solution)/shard_map/dot_general | solution.py:68
  231.6 145.2 %fusion.118 = (f32[16,6144]{1,0:T(8,128)S(1)}, f32[16,6144]{1,0:T(8,128)S(1)}, f32[16,6144]{1,0:T(8,128)S(1)}, f32[16,6144]{1,0:T(8,128)S(1)}) fusion(f32[192,6144]{1,0:T(8,128)} %fusion.4, f32[192,6144]{1,0:T(8,128)} %fusion.6, f32[192,6144]{1,0:T(8,128)} %fusion.8, f32[192,6144]{1,0:T(8,128)} %fusion.10), kind=kCustom, calls=%all-reduce-scatter.4 | all-reduce-scatter fusion | flops 6291457 | bytes 20447744
  384.0 7.0 %collective-permute-start.15 = (f32[12,6144]{1,0:T(8,128)S(1)}, f32[12,6144]{1,0:T(8,128)S(1)}, u32[]{:S(2)}, u32[]{:S(2)}) collective-permute-start(f32[12,6144]{1,0:T(8,128)S(1)} %slice.123), channel_id=1, source_target_pairs={{0,4},{1,5},{2,6},{3,7},{4,8},{5,9},{6,10},{7,11},{8,12},{9,13},{1... | collective-permute-start | bytes 884744
  393.7 10.7 %collective-permute-done.15 = f32[12,6144]{1,0:T(8,128)S(1)} collective-permute-done((f32[12,6144]{1,0:T(8,128)S(1)}, f32[12,6144]{1,0:T(8,128)S(1)}, u32[]{:S(2)}, u32[]{:S(2)}) %collective-permute-start.15) | collective-permute-done | bytes 294944
  406.5 9.7 %collective-permute-start.8 = (f32[16,6144]{1,0:T(8,128)S(1)}, f32[16,6144]{1,0:T(8,128)}, u32[]{:S(2)}, u32[]{:S(2)}) collective-permute-start(f32[16,6144]{1,0:T(8,128)S(1)} %get-tuple-element.17), channel_id=1, source_target_pairs={{0,1},{1,2},{2,3},{3,4},{4,5},{5,6},{6,7},{7,8},{8,9},{9,10},{10,1... | collective-permute-start | bytes 1179656
  416.2 5.9 collective-permute-start.6
  422.1 9.2 %collective-permute-start.11 = (f32[12,6144]{1,0:T(8,128)S(1)}, f32[12,6144]{1,0:T(8,128)}, u32[]{:S(2)}, u32[]{:S(2)}) collective-permute-start(f32[12,6144]{1,0:T(8,128)S(1)} %slice.122), channel_id=1, source_target_pairs={{0,4},{1,5},{2,6},{3,7},{4,8},{5,9},{6,10},{7,11},{8,12},{9,13},{1... | collective-permute-start | bytes 884744
  431.3 18.5 %concatenate.3 = f32[76,6144]{1,0:T(8,128)} concatenate(f32[12,6144]{1,0:T(8,128)} %copy-done.5, f32[16,6144]{1,0:T(8,128)S(1)} %collective-permute-done.14, f32[16,6144]{1,0:T(8,128)} %collective-permute-done.13, f32[16,6144]{1,0:T(8,128)} %collective-permute-done.12, f32[16,6144]{1,0:T(8,128)S(1)} %get-tuple-element.16), dimensions={0} | concatenate | bytes 3735552
  456.1 6.8 %collective-permute-start.7 = (f32[12,6144]{1,0:T(8,128)S(1)}, f32[12,6144]{1,0:T(8,128)}, u32[]{:S(2)}, u32[]{:S(2)}) collective-permute-start(f32[12,6144]{1,0:T(8,128)S(1)} %slice.121), channel_id=1, source_target_pairs={{0,4},{1,5},{2,6},{3,7},{4,8},{5,9},{6,10},{7,11},{8,12},{9,13},{1... | collective-permute-start | bytes 884744
  462.9 18.8 %concatenate.2 = f32[76,6144]{1,0:T(8,128)} concatenate(f32[12,6144]{1,0:T(8,128)} %collective-permute-done.11, f32[16,6144]{1,0:T(8,128)} %collective-permute-done.10, f32[16,6144]{1,0:T(8,128)} %collective-permute-done.9, f32[16,6144]{1,0:T(8,128)} %collective-permute-done.8, f32[16,6144]{1,0:T(8,128)S(1)} %get-tuple-element.17), dimensions={0} | concatenate | bytes 3735552
  492.6 18.5 %concatenate.1 = f32[76,6144]{1,0:T(8,128)} concatenate(f32[12,6144]{1,0:T(8,128)} %collective-permute-done.7, f32[16,6144]{1,0:T(8,128)} %collective-permute-done.6, f32[16,6144]{1,0:T(8,128)S(1)} %collective-permute-done.5, f32[16,6144]{1,0:T(8,128)} %collective-permute-done.4, f32[16,6144]{1,0:T(8,128)S(1)} %get-tuple-element.18), dimensions={0} | concatenate | bytes 3735552
  512.3 18.3 %concatenate = f32[76,6144]{1,0:T(8,128)} concatenate(f32[12,6144]{1,0:T(8,128)} %collective-permute-done.3, f32[16,6144]{1,0:T(8,128)S(1)} %collective-permute-done.2, f32[16,6144]{1,0:T(8,128)S(1)} %collective-permute-done.1, f32[16,6144]{1,0:T(8,128)} %collective-permute-done, f32[16,6144]{1,0:T(8,128)S(1)} %get-tuple-element.19), dimensions={0} | concatenate | bytes 3735552
  542.8 42.9 %reduce-scatter.10.cloned.1.call-done = f32[4,32,768]{2,1,0:T(8,128)} async-done(((f32[4,32,6144]{2,1,0:T(8,128)}), f32[4,32,768]{2,1,0:T(8,128)}) %reduce-scatter.10.cloned.1.call-update) | async-done | bytes 393232 | tf_op jit(solution)/shard_map/reduce_scatter | solution.py:88
  (114 shorter events, 93.5 us)
Async XLA Ops:
  6.5 66.2 %copy-start = (bf16[6144,8]{0,1:T(8,128)(2,1)S(1)}, bf16[6144,8]{0,1:T(8,128)(2,1)}, u32[]{:S(2)}) copy-start(bf16[6144,8]{0,1:T(8,128)(2,1)} %param.11) | copy-start | bytes 294916
  14.5 49.5 %all-to-all-start = ((bf16[16,12,6144]{2,1,0:T(8,128)(2,1)}), bf16[16,12,6144]{2,1,0:T(8,128)(2,1)}, u32[]{:S(2)}, u32[]{:S(2)}) async-start(bf16[16,12,6144]{2,1,0:T(8,128)(2,1)} %stack.18), calls=%async_computation | async-start | bytes 6291456 | tf_op jit(solution)/shard_map/all_to_all | solution.py:61
  66.1 48.4 %all-to-all-start.1 = ((bf16[16,12,6144]{2,1,0:T(8,128)(2,1)}), bf16[16,12,6144]{2,1,0:T(8,128)(2,1)}, u32[]{:S(2)}, u32[]{:S(2)}) async-start(bf16[16,12,6144]{2,1,0:T(8,128)(2,1)} %stack.20), calls=%async_computation.1 | async-start | bytes 6291456 | tf_op jit(solution)/shard_map/all_to_all | solution.py:61
  116.6 48.3 %all-to-all-start.2 = ((bf16[16,12,6144]{2,1,0:T(8,128)(2,1)}), bf16[16,12,6144]{2,1,0:T(8,128)(2,1)S(1)}, u32[]{:S(2)}, u32[]{:S(2)}) async-start(bf16[16,12,6144]{2,1,0:T(8,128)(2,1)} %stack.22), calls=%async_computation.2 | async-start | bytes 6291456 | tf_op jit(solution)/shard_map/all_to_all | solution.py:61
  166.9 48.2 %all-to-all-start.3 = ((bf16[16,12,6144]{2,1,0:T(8,128)(2,1)}), bf16[16,12,6144]{2,1,0:T(8,128)(2,1)}, u32[]{:S(2)}, u32[]{:S(2)}) async-start(bf16[16,12,6144]{2,1,0:T(8,128)(2,1)} %stack.24), calls=%async_computation.3 | async-start | bytes 6291456 | tf_op jit(solution)/shard_map/all_to_all | solution.py:61
  172.7 413.0 %reduce-scatter.10.cloned.1.call-start = ((), (), s32[]{:S(2)}) async-start(), calls=%async_computation.5 | async-start | bytes 3538944 | tf_op jit(solution)/shard_map/reduce_scatter | solution.py:88
  231.6 151.1 %copy-start.8 = (u32[128]{0:T(128)S(1)}, u32[128]{0:T(128)}, u32[]{:S(2)}) copy-start(u32[128]{0:T(128)} %constant.51) | copy-start | bytes 1540
  376.8 29.7 %collective-permute-start.14 = (f32[16,6144]{1,0:T(8,128)S(1)}, f32[16,6144]{1,0:T(8,128)S(1)}, u32[]{:S(2)}, u32[]{:S(2)}) collective-permute-start(f32[16,6144]{1,0:T(8,128)S(1)} %get-tuple-element.16), channel_id=1, source_target_pairs={{0,3},{1,4},{2,5},{3,6},{4,7},{5,8},{6,9},{7,10},{8,11},{9,12},{10... | collective-permute-start | bytes 1179656
  378.1 38.1 %collective-permute-start.13 = (f32[16,6144]{1,0:T(8,128)S(1)}, f32[16,6144]{1,0:T(8,128)}, u32[]{:S(2)}, u32[]{:S(2)}) collective-permute-start(f32[16,6144]{1,0:T(8,128)S(1)} %get-tuple-element.16), channel_id=1, source_target_pairs={{0,2},{1,3},{2,4},{3,5},{4,6},{5,7},{6,8},{7,9},{8,10},{9,11},{10,... | collective-permute-start | bytes 1179656
  380.2 41.9 %collective-permute-start.12 = (f32[16,6144]{1,0:T(8,128)S(1)}, f32[16,6144]{1,0:T(8,128)}, u32[]{:S(2)}, u32[]{:S(2)}) collective-permute-start(f32[16,6144]{1,0:T(8,128)S(1)} %get-tuple-element.16), channel_id=1, source_target_pairs={{0,1},{1,2},{2,3},{3,4},{4,5},{5,6},{6,7},{7,8},{8,9},{9,10},{10,1... | collective-permute-start | bytes 1179656
  384.0 20.5 %collective-permute-start.15 = (f32[12,6144]{1,0:T(8,128)S(1)}, f32[12,6144]{1,0:T(8,128)S(1)}, u32[]{:S(2)}, u32[]{:S(2)}) collective-permute-start(f32[12,6144]{1,0:T(8,128)S(1)} %slice.123), channel_id=1, source_target_pairs={{0,4},{1,5},{2,6},{3,7},{4,8},{5,9},{6,10},{7,11},{8,12},{9,13},{1... | collective-permute-start | bytes 884744
  391.1 61.6 %collective-permute-start.10 = (f32[16,6144]{1,0:T(8,128)S(1)}, f32[16,6144]{1,0:T(8,128)}, u32[]{:S(2)}, u32[]{:S(2)}) collective-permute-start(f32[16,6144]{1,0:T(8,128)S(1)} %get-tuple-element.17), channel_id=1, source_target_pairs={{0,3},{1,4},{2,5},{3,6},{4,7},{5,8},{6,9},{7,10},{8,11},{9,12},{10... | collective-permute-start | bytes 1179656
  404.5 50.3 %collective-permute-start.9 = (f32[16,6144]{1,0:T(8,128)S(1)}, f32[16,6144]{1,0:T(8,128)}, u32[]{:S(2)}, u32[]{:S(2)}) collective-permute-start(f32[16,6144]{1,0:T(8,128)S(1)} %get-tuple-element.17), channel_id=1, source_target_pairs={{0,2},{1,3},{2,4},{3,5},{4,6},{5,7},{6,8},{7,9},{8,10},{9,11},{10,... | collective-permute-start | bytes 1179656
  406.5 49.6 %collective-permute-start.8 = (f32[16,6144]{1,0:T(8,128)S(1)}, f32[16,6144]{1,0:T(8,128)}, u32[]{:S(2)}, u32[]{:S(2)}) collective-permute-start(f32[16,6144]{1,0:T(8,128)S(1)} %get-tuple-element.17), channel_id=1, source_target_pairs={{0,1},{1,2},{2,3},{3,4},{4,5},{5,6},{6,7},{7,8},{8,9},{9,10},{10,1... | collective-permute-start | bytes 1179656
  416.2 68.3 %collective-permute-start.6 = (f32[16,6144]{1,0:T(8,128)S(1)}, f32[16,6144]{1,0:T(8,128)}, u32[]{:S(2)}, u32[]{:S(2)}) collective-permute-start(f32[16,6144]{1,0:T(8,128)S(1)} %get-tuple-element.18), channel_id=1, source_target_pairs={{0,3},{1,4},{2,5},{3,6},{4,7},{5,8},{6,9},{7,10},{8,11},{9,12},{10... | collective-permute-start | bytes 1179656
  422.1 28.8 %collective-permute-start.11 = (f32[12,6144]{1,0:T(8,128)S(1)}, f32[12,6144]{1,0:T(8,128)}, u32[]{:S(2)}, u32[]{:S(2)}) collective-permute-start(f32[12,6144]{1,0:T(8,128)S(1)} %slice.122), channel_id=1, source_target_pairs={{0,4},{1,5},{2,6},{3,7},{4,8},{5,9},{6,10},{7,11},{8,12},{9,13},{1... | collective-permute-start | bytes 884744
  450.9 36.7 %collective-permute-start.5 = (f32[16,6144]{1,0:T(8,128)S(1)}, f32[16,6144]{1,0:T(8,128)S(1)}, u32[]{:S(2)}, u32[]{:S(2)}) collective-permute-start(f32[16,6144]{1,0:T(8,128)S(1)} %get-tuple-element.18), channel_id=1, source_target_pairs={{0,2},{1,3},{2,4},{3,5},{4,6},{5,7},{6,8},{7,9},{8,10},{9,11},{10,... | collective-permute-start | bytes 1179656
  452.7 39.9 %collective-permute-start.4 = (f32[16,6144]{1,0:T(8,128)S(1)}, f32[16,6144]{1,0:T(8,128)}, u32[]{:S(2)}, u32[]{:S(2)}) collective-permute-start(f32[16,6144]{1,0:T(8,128)S(1)} %get-tuple-element.18), channel_id=1, source_target_pairs={{0,1},{1,2},{2,3},{3,4},{4,5},{5,6},{6,7},{7,8},{8,9},{9,10},{10,1... | collective-permute-start | bytes 1179656
  454.8 57.5 %collective-permute-start.2 = (f32[16,6144]{1,0:T(8,128)S(1)}, f32[16,6144]{1,0:T(8,128)S(1)}, u32[]{:S(2)}, u32[]{:S(2)}) collective-permute-start(f32[16,6144]{1,0:T(8,128)S(1)} %get-tuple-element.19), channel_id=1, source_target_pairs={{0,3},{1,4},{2,5},{3,6},{4,7},{5,8},{6,9},{7,10},{8,11},{9,12},{10... | collective-permute-start | bytes 1179656
  456.1 26.7 %collective-permute-start.7 = (f32[12,6144]{1,0:T(8,128)S(1)}, f32[12,6144]{1,0:T(8,128)}, u32[]{:S(2)}, u32[]{:S(2)}) collective-permute-start(f32[12,6144]{1,0:T(8,128)S(1)} %slice.121), channel_id=1, source_target_pairs={{0,4},{1,5},{2,6},{3,7},{4,8},{5,9},{6,10},{7,11},{8,12},{9,13},{1... | collective-permute-start | bytes 884744
  482.7 29.5 %collective-permute-start.1 = (f32[16,6144]{1,0:T(8,128)S(1)}, f32[16,6144]{1,0:T(8,128)S(1)}, u32[]{:S(2)}, u32[]{:S(2)}) collective-permute-start(f32[16,6144]{1,0:T(8,128)S(1)} %get-tuple-element.19), channel_id=1, source_target_pairs={{0,2},{1,3},{2,4},{3,5},{4,6},{5,7},{6,8},{7,9},{8,10},{9,11},{10,... | collective-permute-start | bytes 1179656
  484.5 27.8 %collective-permute-start = (f32[16,6144]{1,0:T(8,128)S(1)}, f32[16,6144]{1,0:T(8,128)}, u32[]{:S(2)}, u32[]{:S(2)}) collective-permute-start(f32[16,6144]{1,0:T(8,128)S(1)} %get-tuple-element.19), channel_id=1, source_target_pairs={{0,1},{1,2},{2,3},{3,4},{4,5},{5,6},{6,7},{7,8},{8,9},{9,10},{10,1... | collective-permute-start | bytes 1179656
  487.6 24.7 %collective-permute-start.3 = (f32[12,6144]{1,0:T(8,128)S(1)}, f32[12,6144]{1,0:T(8,128)}, u32[]{:S(2)}, u32[]{:S(2)}) collective-permute-start(f32[12,6144]{1,0:T(8,128)S(1)} %slice.120), channel_id=1, source_target_pairs={{0,4},{1,5},{2,6},{3,7},{4,8},{5,9},{6,10},{7,11},{8,12},{9,13},{1... | collective-permute-start | bytes 884744
  540.8 46.8 %copy-start.1 = (bf16[6144,8]{0,1:T(8,128)(2,1)S(1)}, bf16[6144,8]{0,1:T(8,128)(2,1)}, u32[]{:S(2)}) copy-start(bf16[6144,8]{0,1:T(8,128)(2,1)} %param.11) | copy-start | bytes 294916
  (6 other events, 41.5 us)
Sparse Core Ops, SparseCore 0:
  539.5 46.1 reduce-scatter.9
